TPU v7x, 128 devices: a whole 4x4x4 slice. The times are simulated.
128 devices in a mesh: grid: 64 (over x, y, z_lo, core), col: 2 (over z_hi).
Axes of the slice: x: 4, y: 4, z: 4 (z_hi: 2, z_lo: 2; z = z_hi * 2 + z_lo), core: 2. Of those that a mesh axis runs over, the one named last changes fastest.
Arguments:
- orbitals: bfloat16 [884736, 256], P(('grid', 'col')), may hold values from -6 to 6
- points: int32 [1024], replicated, may hold values from 0 to 884735, as said below
- cinv: bfloat16 [1024, 256], replicated, may hold values from -0.1875 to 0.1875
Outputs:
- potential: bfloat16 [256, 884736], P(None, ('grid', 'col'))
- coupling: float32 [1024, 256], P(('grid', 'col'))
Inputs may be any that keep to these rules, and one draw needn't show every extreme that they name: `points`: 1024 distinct grid rows.
All inputs are finite; a program needn't handle non-finite values.
Results may differ from a plain program's by a relative error of at most 0.0046.
Values may be sent and summed in bfloat16 or wider, within the bound.
A program may use at most 192 MiB of HBM per device.

v0:
```python
import math
import jax
import jax.numpy as jnp
from jax import lax
from jax.sharding import PartitionSpec as P

NX = 96
screening = 0.25


def kernel_table(size):
    index = jnp.arange(size)
    wave = jnp.where(index < (size + 1) // 2, index, index - size).astype(jnp.float32) * (
        2.0 * math.pi / size
    )
    squared = wave[:, None, None] ** 2 + wave[None, :, None] ** 2 + wave[None, None, :] ** 2
    return jnp.where(squared > 0, 1.0 / (squared + screening), 0.0)


def along(table, values, axis):
    forms = {1: "kn,cnyz->ckyz", 2: "kn,cxnz->cxkz", 3: "kn,cxyn->cxyk"}
    return jnp.einsum(forms[axis], table, values, precision=lax.Precision.HIGHEST)


def screened_solve(field):
    size = field.shape[1]
    index = jnp.arange(size, dtype=jnp.int32)
    phase = index[:, None] * index[None, :] % size
    angle = phase.astype(jnp.float32) * (2.0 * math.pi / size)
    cos_table = jnp.cos(angle)
    sin_table = jnp.sin(angle)
    real_part = along(cos_table, field, 3)
    imag_part = -along(sin_table, field, 3)
    for axis in (2, 1):
        real_part, imag_part = (
            along(cos_table, real_part, axis) + along(sin_table, imag_part, axis),
            along(cos_table, imag_part, axis) - along(sin_table, real_part, axis),
        )
    weights = kernel_table(size)
    real_part = real_part * weights
    imag_part = imag_part * weights
    for axis in (1, 2):
        real_part, imag_part = (
            along(cos_table, real_part, axis) - along(sin_table, imag_part, axis),
            along(cos_table, imag_part, axis) + along(sin_table, real_part, axis),
        )
    result = along(cos_table, real_part, 3) - along(sin_table, imag_part, 3)
    return result / float(size**3)


def local(orbitals, points, cinv):
    ranks = lax.axis_size(("grid", "col"))
    local_rows = orbitals.shape[0]
    orbital_count = orbitals.shape[1]
    npoints = cinv.shape[0]
    columns = cinv.shape[1]
    per_rank = columns // ranks
    first_row = lax.axis_index(("grid", "col")) * local_rows
    offset = points - first_row
    inside = (offset >= 0) & (offset < local_rows)
    picked = jnp.take(orbitals, jnp.clip(offset, 0, local_rows - 1), axis=0)
    picked = jnp.where(inside[:, None], picked.astype(jnp.float32), 0.0)
    point_rows = lax.psum(picked, ("grid", "col")).astype(jnp.bfloat16)
    scale = 1.0 / math.sqrt(orbital_count)
    block_rows = math.gcd(local_rows, 1152)

    def pair_block(block):
        product = (
            lax.dot_general(
                block, point_rows, (((1,), (1,)), ((), ())), preferred_element_type=jnp.float32
            )
            * scale
        )
        return (product * product).astype(jnp.bfloat16)

    pairs = lax.map(
        pair_block, orbitals.reshape(local_rows // block_rows, block_rows, orbital_count)
    )
    pairs = pairs.reshape(local_rows, npoints)
    theta_cols = lax.dot_general(
        cinv, pairs, (((0,), (1,)), ((), ())), preferred_element_type=jnp.float32
    )
    fields = lax.all_to_all(theta_cols, ("grid", "col"), split_axis=0, concat_axis=1, tiled=True)
    fields = fields.reshape(per_rank, NX, NX, NX)
    potentials = screened_solve(fields).astype(jnp.bfloat16).reshape(per_rank, NX * NX * NX)
    rows_back = lax.all_to_all(potentials, ("grid", "col"), split_axis=1, concat_axis=0, tiled=True)
    factor = math.sqrt(npoints) / float(NX**3)
    coupling = lax.psum_scatter(
        lax.dot_general(
            pairs, rows_back, (((0,), (1,)), ((), ())), preferred_element_type=jnp.float32
        )
        * factor,
        ("grid", "col"),
        scatter_dimension=0,
        tiled=True,
    )
    return (rows_back, coupling)


def solution(mesh):
    in_specs = (P(("grid", "col"), None), P(), P())
    out_specs = (P(None, ("grid", "col")), P(("grid", "col"), None))
    return jax.shard_map(local, mesh=mesh, in_specs=in_specs, out_specs=out_specs, check_vma=False)
```

profile of v0, /device:TPU:0, one launch (start us, length us, event | category | flops | bytes accessed | tf_op | source)
XLA Modules:
  0.0 1324.5 jit_solution(9655108853187020111)
XLA Ops:
  7.2 0.0 copy-start
  7.2 0.8 compare_and_fusion.1
  7.9 0.7 fusion.144
  8.6 5.9 gather_fusion
  14.6 0.3 convert_select_fusion
  14.9 74.1 %all-reduce.1 = bf16[1024,256]{1,0:T(8,128)(2,1)S(1)} all-reduce(f32[1024,256]{1,0:T(8,128)S(1)} %convert_select_fusion), channel_id=1, replica_groups=mesh['grid'=64,'col'=2] {'grid','col'}, use_global_device_ids=true, to_apply=%region_0.1 | all-reduce | flops 262144 | bytes 1572864 | tf_op jit(solution)/shard_map/psum | solution.py:63
  89.0 19.9 %while.10 = (s32[]{:T(128)}, bf16[6,1152,1024]{2,1,0:T(8,128)(2,1)}, bf16[6,1152,256]{2,1,0:T(8,128)(2,1)}, bf16[1024,256]{1,0:T(8,128)(2,1)S(1)}, s32[]{:T(128)}) while((s32[]{:T(128)}, bf16[6,1152,1024]{2,1,0:T(8,128)(2,1)}, bf16[6,1152,256]{2,1,0:T(8,128)(2,1)}, bf16[1024,256]{1,0:T(8,128)(2,1)S(1)}, s32[]{:T(128)}) %tuple.28), condition=%wide.region_2.3_spmd, body=%wide.region_1.2_spmd.sunk | while | flops 607518720 | bytes 3474501 | solution.py:76
  89.0 3.3 fusion.234
  92.3 3.3 fusion.234
  95.7 3.3 fusion.234
  99.0 3.4 fusion.234
  102.3 3.3 fusion.234
  105.6 3.3 fusion.234
  109.0 0.0 copy-done
  109.0 11.7 convolution_bitcast_fusion
  120.7 9.1 all_to_all.26
  129.8 6.9 all-to-all-start
  136.7 0.3 reduce-scatter.2.cloned.1.call-start
  137.0 0.1 broadcast_add_fusion
  137.1 3.1 fusion.18
  140.1 81.1 %all-to-all-done = f32[128,2,6912]{2,1,0:T(2,128)} async-done(((f32[128,2,6912]{2,1,0:T(2,128)}), f32[128,2,6912]{2,1,0:T(2,128)}, u32[]{:S(2)}, u32[]{:S(2)}) %all-to-all-start) | async-done | bytes 7077920 | tf_op jit(solution)/shard_map/all_to_all | solution.py:83
  221.2 6.4 copy.15
  227.6 10.6 reshape.103
  238.2 11.3 fusion.39
  249.5 0.0 copy-done.6
  249.5 21.2 %fusion.57 = f32[2,96,96,96]{2,3,1,0:T(8,128)S(1)} fusion(f32[2,96,96,96]{3,2,1,0:T(8,128)S(1)} %copy-done.6), kind=kOutput, calls=%fused_computation.66 | convolution fusion | flops 2038514688 | bytes 14155776 | tf_op jit(solution)/shard_map/kn,cxyn->cxyk/dot_general | solution.py:22
  270.7 8.8 fusion.55
  279.5 10.5 fusion.36
  290.0 19.2 %subtract_bitcast_fusion.1 = f32[2,96,96,96]{2,3,1,0:T(8,128)} fusion(f32[2,96,96,96]{3,2,1,0:T(8,128)} %fusion.36, f32[2,96,96,96]{3,2,1,0:T(8,128)S(1)} %fusion.39), kind=kOutput, calls=%fused_computation.21 | convolution fusion | flops 2042053632 | bytes 21233664 | tf_op jit(solution)/shard_map/kn,cxnz->cxkz/dot_general | solution.py:22
  309.2 17.8 %add_bitcast_fusion.1 = f32[2,96,96,96]{2,3,1,0:T(8,128)} fusion(f32[2,96,96,96]{3,2,1,0:T(8,128)S(1)} %fusion.55, f32[2,96,96,96]{3,2,1,0:T(8,128)S(1)} %fusion.39), kind=kOutput, calls=%fused_computation.22 | convolution fusion | flops 2042053632 | bytes 21233664 | tf_op jit(solution)/shard_map/kn,cxnz->cxkz/dot_general | solution.py:22
  326.9 12.4 copy.18
  339.3 12.4 copy.21
  351.7 13.4 %fusion.48 = f32[2,96,96,96]{3,2,1,0:T(8,128)} fusion(f32[2,96,96,96]{1,3,2,0:T(8,128)} %copy.21), kind=kOutput, calls=%fused_computation.57 | convolution fusion | flops 2038514688 | bytes 14155776 | tf_op jit(solution)/shard_map/kn,cnyz->ckyz/dot_general | solution.py:22
  365.1 0.0 copy-done.5
  365.1 10.2 fusion.53
  375.3 0.0 slice-done
  375.3 0.0 slice-done.1
  375.3 11.3 bitcast_multiply_fusion
  386.6 0.0 copy-start.2
  386.6 15.4 %bitcast_multiply_fusion.1 = f32[2,96,96,96]{1,3,2,0:T(8,128)S(1)} fusion(f32[2,96,96,96]{3,2,1,0:T(8,128)} %fusion.53, f32[96,96,96]{0,2,1:T(8,128)S(1)} %bitcast.109, f32[2,96,96,96]{1,3,2,0:T(8,128)} %copy.21), kind=kOutput, calls=%fused_computation.15 | convolution fusion | flops 2042053632 | bytes 24772608 | tf_op jit(solution)/shard_map/kn,cnyz->ckyz/dot_general | solution.py:22
  402.0 10.3 fusion.50
  412.3 0.0 copy-done.2
  412.3 8.8 fusion.44
  421.1 10.6 add_bitcast_fusion
  431.7 12.4 copy.31
  444.1 0.0 slice-start.6
  444.1 26.4 %fusion.41 = f32[2,96,96,96]{2,3,1,0:T(8,128)} fusion(f32[2,96,96,96]{2,3,1,0:T(8,128)} %copy.31), kind=kOutput, calls=%fused_computation.50 | convolution fusion | flops 2038514688 | bytes 14155776 | tf_op jit(solution)/shard_map/kn,cxnz->cxkz/dot_general | solution.py:22
  470.6 0.0 copy-done.3
  470.6 23.6 %fusion.30 = f32[2,96,96,96]{2,3,1,0:T(8,128)} fusion(f32[2,96,96,96]{2,3,1,0:T(8,128)S(1)} %copy-done.3), kind=kOutput, calls=%fused_computation.39 | convolution fusion | flops 2038514688 | bytes 14155776 | tf_op jit(solution)/shard_map/kn,cxnz->cxkz/dot_general | solution.py:22
  494.2 0.0 slice-done.3
  494.3 10.6 subtract_bitcast_fusion
  504.8 12.5 copy.30
  517.4 24.6 %fusion.28 = f32[2,96,96,96]{2,3,1,0:T(8,128)S(1)} fusion(f32[2,96,96,96]{2,3,1,0:T(8,128)} %copy.30), kind=kOutput, calls=%fused_computation.37 | convolution fusion | flops 2038514688 | bytes 14155776 | tf_op jit(solution)/shard_map/kn,cxnz->cxkz/dot_general | solution.py:22
  542.0 0.0 slice-start.10
  542.0 23.4 %fusion.46 = f32[2,96,96,96]{2,3,1,0:T(8,128)} fusion(f32[2,96,96,96]{2,3,1,0:T(8,128)S(1)} %copy-done.4), kind=kOutput, calls=%fused_computation.55 | convolution fusion | flops 2038514688 | bytes 14155776 | tf_op jit(solution)/shard_map/kn,cxnz->cxkz/dot_general | solution.py:22
  565.4 10.2 fusion.7
  575.6 15.9 %multiply_convert_fusion = bf16[2,96,96,96]{3,2,1,0:T(8,128)(2,1)} fusion(f32[2,96,96,96]{3,2,1,0:T(8,128)} %fusion.7, f32[2,96,96,96]{2,3,1,0:T(8,128)} %fusion.46, f32[2,96,96,96]{2,3,1,0:T(8,128)} %fusion.30), kind=kOutput, calls=%fused_computation.16 | convolution fusion | flops 2045592576 | bytes 24772608 | tf_op jit(solution)/shard_map/kn,cxyn->cxyk/dot_general | solution.py:22
  591.5 7.8 all_to_all.29
  599.3 5.6 copy.24
  604.9 55.8 %all_to_all.35 = bf16[2,128,6912]{2,0,1:T(2,128)(2,1)} all-to-all(bf16[2,128,6912]{2,0,1:T(2,128)(2,1)S(1)} %copy.24), channel_id=1, replica_groups=mesh['grid'=64,'col'=2] {'grid','col'}, dimensions={1} | all-to-all | bytes 7077888 | tf_op jit(solution)/shard_map/all_to_all | solution.py:86
  660.7 8.3 all_to_all.32
  669.0 10.9 convolution_multiply_fusion.1
  679.9 0.0 reduce-scatter.2.cloned.1.call-update
  679.9 637.2 %reduce-scatter.2.cloned.1.call-done = f32[8,256]{1,0:T(8,128)} async-done(((f32[1024,256]{1,0:T(8,128)}), f32[8,256]{1,0:T(8,128)}) %reduce-scatter.2.cloned.1.call-update) | async-done | bytes 8208 | tf_op jit(solution)/shard_map/reduce_scatter | solution.py:88
  (30 shorter events, 0.1 us)
Async XLA Ops:
  7.2 101.8 %copy-start = (bf16[1024,256]{1,0:T(8,128)(2,1)S(1)}, bf16[1024,256]{1,0:T(8,128)(2,1)}, u32[]{:S(2)}) copy-start(bf16[1024,256]{1,0:T(8,128)(2,1)} %param.7) | copy-start | bytes 1572868
  129.8 91.4 %all-to-all-start = ((f32[128,2,6912]{2,1,0:T(2,128)}), f32[128,2,6912]{2,1,0:T(2,128)}, u32[]{:S(2)}, u32[]{:S(2)}) async-start(f32[128,2,6912]{2,1,0:T(2,128)} %all_to_all.26), calls=%async_computation | async-start | bytes 14155776 | tf_op jit(solution)/shard_map/all_to_all | solution.py:83
  136.7 1180.5 %reduce-scatter.2.cloned.1.call-start = ((), (), s32[]{:S(2)}) async-start(), calls=%async_computation.3 | async-start | bytes 1056768 | tf_op jit(solution)/shard_map/reduce_scatter | solution.py:88
  238.2 11.3 copy-start.6
  351.7 13.4 %copy-start.5 = (f32[2,96,96,96]{1,3,2,0:T(8,128)S(1)}, f32[2,96,96,96]{1,3,2,0:T(8,128)}, u32[]{:S(2)}) copy-start(f32[2,96,96,96]{1,3,2,0:T(8,128)} %copy.18) | copy-start | bytes 21233668
  351.7 23.6 %slice-start = ((s8[4718592]{0:T(1024)(128)(4,1)}), s8[4194304]{0:T(1024)(128)(4,1)S(1)}, s32[]{:S(2)}) async-start(s8[4718592]{0:T(1024)(128)(4,1)} %bitcast.108), calls=%async_computation.4 | async-start | bytes 8388608
  365.1 10.2 slice-start.1
  386.6 25.7 %copy-start.2 = (f32[2,96,96,96]{1,3,2,0:T(8,128)}, f32[2,96,96,96]{1,3,2,0:T(8,128)S(1)}, u32[]{:S(2)}) copy-start(f32[2,96,96,96]{1,3,2,0:T(8,128)S(1)} %bitcast_multiply_fusion) | copy-start | bytes 21233668
  444.1 26.4 %copy-start.3 = (f32[2,96,96,96]{2,3,1,0:T(8,128)S(1)}, f32[2,96,96,96]{2,3,1,0:T(8,128)}, u32[]{:S(2)}) copy-start(f32[2,96,96,96]{2,3,1,0:T(8,128)} %copy.31) | copy-start | bytes 21233668
  444.1 50.1 %slice-start.2 = ((s8[9437184]{0:T(1024)(128)(4,1)}), s8[4194304]{0:T(1024)(128)(4,1)S(1)}, s32[]{:S(2)}) async-start(s8[9437184]{0:T(1024)(128)(4,1)} %bitcast.110), calls=%async_computation.6 | async-start | bytes 8388608
  444.1 50.1 %slice-start.3 = ((s8[9437184]{0:T(1024)(128)(4,1)}), s8[4194304]{0:T(1024)(128)(4,1)S(1)}, s32[]{:S(2)}) async-start(s8[9437184]{0:T(1024)(128)(4,1)} %bitcast.110), calls=%async_computation.7 | async-start | bytes 8388608
  444.1 50.1 %slice-start.5 = ((s8[9437184]{0:T(1024)(128)(4,1)}), s8[4194304]{0:T(1024)(128)(4,1)S(1)}, s32[]{:S(2)}) async-start(s8[9437184]{0:T(1024)(128)(4,1)} %bitcast.112), calls=%async_computation.9 | async-start | bytes 8388608
  444.1 50.1 %slice-start.6 = ((s8[9437184]{0:T(1024)(128)(4,1)}), s8[4194304]{0:T(1024)(128)(4,1)S(1)}, s32[]{:S(2)}) async-start(s8[9437184]{0:T(1024)(128)(4,1)} %bitcast.112), calls=%async_computation.10 | async-start | bytes 8388608
  470.6 23.7 %slice-start.4 = ((s8[9437184]{0:T(1024)(128)(4,1)}), s8[1048576]{0:T(1024)(128)(4,1)S(1)}, s32[]{:S(2)}) async-start(s8[9437184]{0:T(1024)(128)(4,1)} %bitcast.110), calls=%async_computation.8 | async-start | bytes 2097152
  470.6 23.7 %slice-start.7 = ((s8[9437184]{0:T(1024)(128)(4,1)}), s8[1048576]{0:T(1024)(128)(4,1)S(1)}, s32[]{:S(2)}) async-start(s8[9437184]{0:T(1024)(128)(4,1)} %bitcast.112), calls=%async_computation.11 | async-start | bytes 2097152
  517.4 24.6 %copy-start.4 = (f32[2,96,96,96]{2,3,1,0:T(8,128)S(1)}, f32[2,96,96,96]{2,3,1,0:T(8,128)}, u32[]{:S(2)}) copy-start(f32[2,96,96,96]{2,3,1,0:T(8,128)} %copy.30) | copy-start | bytes 21233668
  517.4 48.0 %slice-start.8 = ((s8[9437184]{0:T(1024)(128)(4,1)}), s8[4194304]{0:T(1024)(128)(4,1)S(1)}, s32[]{:S(2)}) async-start(s8[9437184]{0:T(1024)(128)(4,1)} %bitcast.114), calls=%async_computation.12 | async-start | bytes 8388608
  517.4 48.0 %slice-start.9 = ((s8[9437184]{0:T(1024)(128)(4,1)}), s8[4194304]{0:T(1024)(128)(4,1)S(1)}, s32[]{:S(2)}) async-start(s8[9437184]{0:T(1024)(128)(4,1)} %bitcast.114), calls=%async_computation.13 | async-start | bytes 8388608
  542.0 23.4 %slice-start.10 = ((s8[9437184]{0:T(1024)(128)(4,1)}), s8[1048576]{0:T(1024)(128)(4,1)S(1)}, s32[]{:S(2)}) async-start(s8[9437184]{0:T(1024)(128)(4,1)} %bitcast.114), calls=%async_computation.14 | async-start | bytes 2097152
  660.7 656.4 %copy-start.1 = (bf16[1024,256]{1,0:T(8,128)(2,1)S(1)}, bf16[1024,256]{1,0:T(8,128)(2,1)}, u32[]{:S(2)}) copy-start(bf16[1024,256]{1,0:T(8,128)(2,1)} %param.7) | copy-start | bytes 1572868
Sparse Core Ops, SparseCore 0:
  680.1 637.0 reduce-scatter.1
where the time goes:
time: 1330 us; the launch traced here: 1320 us
  waiting for transfers between devices  718 us (54%)
  matrix products  346 us (26%)
  blocking collectives  130 us (10%)
  local copies, waits for them, and re-layouts  103 us (8%)
  between operations  14.8 us (1%)
    reduce_scatter x1, waiting for transfers between devices, local(): lax.psum_scatter(lax.dot_general(pairs, rows_back, (((0,), (1,)), ((), ()...  637 us
    dot_general x20, matrix products, along(): jnp.einsum(forms[axis], table, values, precision=lax.Precision.HIGHEST)  303 us
    all_to_all x1, waiting for transfers between devices, local(): lax.all_to_all(theta_cols, ('grid', 'col'), split_axis=0, concat_axis=1,...  81.1 us
    psum x1, blocking collectives, local(): point_rows = lax.psum(picked, ('grid', 'col')).astype(jnp.bfloat16)  74.1 us
    all_to_all x1, blocking collectives, local(): lax.all_to_all(potentials, ('grid', 'col'), split_axis=1, concat_axis=0,...  55.8 us
  transfers between devices with their start and end apart: 2, of which 2 were waited for; matrix products, arithmetic and copies ran while one was open for 0% of the time, Pallas kernels for 0%

commit v1 on v0

--- a/solution.py
+++ b/solution.py
@@ -60,7 +60,7 @@
     inside = (offset >= 0) & (offset < local_rows)
     picked = jnp.take(orbitals, jnp.clip(offset, 0, local_rows - 1), axis=0)
     picked = jnp.where(inside[:, None], picked.astype(jnp.float32), 0.0)
-    point_rows = lax.psum(picked, ("grid", "col")).astype(jnp.bfloat16)
+    point_rows = lax.psum(lax.psum(picked, "grid"), "col").astype(jnp.bfloat16)
     scale = 1.0 / math.sqrt(orbital_count)
     block_rows = math.gcd(local_rows, 1152)
 

time: 1330 us -> 1840 us (1.38)
  waiting for transfers between devices: 718 us -> 1270 us
  blocking collectives: 130 us -> 87.8 us
    psum x0 -> x1, waiting for transfers between devices: none -> 549 us  [local(): point_rows = lax.psum(lax.psum(picked, 'grid'), 'col').astype(jnp.bfloat16)]
    psum x1, blocking collectives: 74.1 us -> 32 us  [local(): point_rows = lax.psum(lax.psum(picked, 'grid'), 'col').astype(jnp.bfloat16)]
  transfers between devices with their start and end apart: 2 -> 3, of which waited for: 2 -> 3; matrix products, arithmetic and copies ran while one was open for 0% -> 0% of each run, Pallas kernels for 0% -> 0%
where the time goes in v1:
time: 1840 us
  waiting for transfers between devices  1270 us (69%)
  matrix products  346 us (19%)
  local copies, waits for them, and re-layouts  103 us (6%)
  blocking collectives  87.8 us (5%)
    reduce_scatter x1, waiting for transfers between devices, local(): lax.psum_scatter(lax.dot_general(pairs, rows_back, (((0,), (1,)), ((), ()...  637 us
    psum x1, waiting for transfers between devices, local(): point_rows = lax.psum(lax.psum(picked, 'grid'), 'col').astype(jnp.bfloat16)  549 us
    dot_general x20, matrix products, along(): jnp.einsum(forms[axis], table, values, precision=lax.Precision.HIGHEST)  303 us
    all_to_all x1, waiting for transfers between devices, local(): lax.all_to_all(theta_cols, ('grid', 'col'), split_axis=0, concat_axis=1,...  81.1 us
    all_to_all x1, blocking collectives, local(): lax.all_to_all(potentials, ('grid', 'col'), split_axis=1, concat_axis=0,...  55.8 us
  transfers between devices with their start and end apart: 3, of which 3 were waited for; matrix products, arithmetic and copies ran while one was open for 0% of the time, Pallas kernels for 0%

profile of v1, /device:TPU:0, one launch (start us, length us, event | category | flops | bytes accessed | tf_op | source)
XLA Modules:
  0.0 1835.6 jit_solution(16731971945219847615)
XLA Ops:
  7.2 0.0 copy-start
  7.2 0.0 all-reduce.3.cloned.1.call-start
  7.2 0.7 compare_and_fusion.1
  8.0 0.7 fusion.144
  8.7 5.9 gather_fusion
  14.6 1.3 convert_select_fusion
  15.9 0.0 all-reduce.3.cloned.1.call-update
  15.9 549.4 %all-reduce.3.cloned.1.call-done = f32[1024,256]{1,0:T(8,128)} async-done(((f32[1024,256]{1,0:T(8,128)}), f32[1024,256]{1,0:T(8,128)}) %all-reduce.3.cloned.1.call-update) | async-done | bytes 1048592 | tf_op jit(solution)/shard_map/psum | solution.py:63
  565.3 32.0 %all-reduce.4 = bf16[1024,256]{1,0:T(8,128)(2,1)S(1)} all-reduce(f32[1024,256]{1,0:T(8,128)} %all-reduce.3.cloned.1.call-done), channel_id=1, replica_groups=mesh['grid'=64,'col'=2] {'col'}, use_global_device_ids=true, to_apply=%region_1.2 | all-reduce | flops 262144 | bytes 1572864 | tf_op jit(solution)/shard_map/psum | solution.py:63
  597.3 19.9 %while.10 = (s32[]{:T(128)}, bf16[6,1152,1024]{2,1,0:T(8,128)(2,1)}, bf16[6,1152,256]{2,1,0:T(8,128)(2,1)}, bf16[1024,256]{1,0:T(8,128)(2,1)S(1)}, s32[]{:T(128)}) while((s32[]{:T(128)}, bf16[6,1152,1024]{2,1,0:T(8,128)(2,1)}, bf16[6,1152,256]{2,1,0:T(8,128)(2,1)}, bf16[1024,256]{1,0:T(8,128)(2,1)S(1)}, s32[]{:T(128)}) %tuple.30), condition=%wide.region_3.4_spmd, body=%wide.region_2.3_spmd.sunk | while | flops 607518720 | bytes 3474501 | solution.py:76
  597.3 3.3 fusion.234
  600.6 3.3 fusion.234
  603.9 3.3 fusion.234
  607.3 3.4 fusion.234
  610.6 3.3 fusion.234
  613.9 3.3 fusion.234
  617.2 0.0 copy-done
  617.2 11.7 convolution_bitcast_fusion
  629.0 9.1 all_to_all.26
  638.1 9.7 all-to-all-start
  647.7 0.3 reduce-scatter.2.cloned.1.call-start
  648.0 0.1 broadcast_add_fusion
  648.1 3.1 fusion.18
  651.2 81.1 %all-to-all-done = f32[128,2,6912]{2,1,0:T(2,128)} async-done(((f32[128,2,6912]{2,1,0:T(2,128)}), f32[128,2,6912]{2,1,0:T(2,128)}, u32[]{:S(2)}, u32[]{:S(2)}) %all-to-all-start) | async-done | bytes 7077920 | tf_op jit(solution)/shard_map/all_to_all | solution.py:83
  732.3 6.4 copy.15
  738.6 10.6 reshape.103
  749.2 11.3 fusion.39
  760.5 0.0 copy-done.6
  760.5 21.2 %fusion.57 = f32[2,96,96,96]{2,3,1,0:T(8,128)S(1)} fusion(f32[2,96,96,96]{3,2,1,0:T(8,128)S(1)} %copy-done.6), kind=kOutput, calls=%fused_computation.66 | convolution fusion | flops 2038514688 | bytes 14155776 | tf_op jit(solution)/shard_map/kn,cxyn->cxyk/dot_general | solution.py:22
  781.8 8.8 fusion.55
  790.6 10.5 fusion.36
  801.0 19.2 %subtract_bitcast_fusion.1 = f32[2,96,96,96]{2,3,1,0:T(8,128)} fusion(f32[2,96,96,96]{3,2,1,0:T(8,128)} %fusion.36, f32[2,96,96,96]{3,2,1,0:T(8,128)S(1)} %fusion.39), kind=kOutput, calls=%fused_computation.21 | convolution fusion | flops 2042053632 | bytes 21233664 | tf_op jit(solution)/shard_map/kn,cxnz->cxkz/dot_general | solution.py:22
  820.2 17.8 add_bitcast_fusion.1
  838.0 12.4 copy.18
  850.3 12.4 copy.21
  862.7 13.4 fusion.48
  876.1 0.0 copy-done.5
  876.1 10.2 fusion.53
  886.3 0.0 slice-done
  886.3 0.0 slice-done.1
  886.3 11.3 bitcast_multiply_fusion
  897.6 15.4 bitcast_multiply_fusion.1
  913.0 10.3 fusion.50
  923.3 8.8 fusion.44
  932.1 10.6 add_bitcast_fusion
  942.8 12.4 copy.31
  955.2 0.0 slice-start.6
  955.2 26.4 %fusion.41 = f32[2,96,96,96]{2,3,1,0:T(8,128)} fusion(f32[2,96,96,96]{2,3,1,0:T(8,128)} %copy.31), kind=kOutput, calls=%fused_computation.50 | convolution fusion | flops 2038514688 | bytes 14155776 | tf_op jit(solution)/shard_map/kn,cxnz->cxkz/dot_general | solution.py:22
  981.6 23.6 %fusion.30 = f32[2,96,96,96]{2,3,1,0:T(8,128)} fusion(f32[2,96,96,96]{2,3,1,0:T(8,128)S(1)} %copy-done.3), kind=kOutput, calls=%fused_computation.39 | convolution fusion | flops 2038514688 | bytes 14155776 | tf_op jit(solution)/shard_map/kn,cxnz->cxkz/dot_general | solution.py:22
  1005.2 0.0 slice-done.3
  1005.3 10.6 subtract_bitcast_fusion
  1015.9 12.5 copy.30
  1028.4 24.6 %fusion.28 = f32[2,96,96,96]{2,3,1,0:T(8,128)S(1)} fusion(f32[2,96,96,96]{2,3,1,0:T(8,128)} %copy.30), kind=kOutput, calls=%fused_computation.37 | convolution fusion | flops 2038514688 | bytes 14155776 | tf_op jit(solution)/shard_map/kn,cxnz->cxkz/dot_general | solution.py:22
  1053.0 0.0 slice-start.10
  1053.0 23.4 %fusion.46 = f32[2,96,96,96]{2,3,1,0:T(8,128)} fusion(f32[2,96,96,96]{2,3,1,0:T(8,128)S(1)} %copy-done.4), kind=kOutput, calls=%fused_computation.55 | convolution fusion | flops 2038514688 | bytes 14155776 | tf_op jit(solution)/shard_map/kn,cxnz->cxkz/dot_general | solution.py:22
  1076.4 10.2 fusion.7
  1086.7 15.9 multiply_convert_fusion
  1102.6 7.8 all_to_all.29
  1110.3 5.6 copy.24
  1116.0 55.8 %all_to_all.35 = bf16[2,128,6912]{2,0,1:T(2,128)(2,1)} all-to-all(bf16[2,128,6912]{2,0,1:T(2,128)(2,1)S(1)} %copy.24), channel_id=1, replica_groups=mesh['grid'=64,'col'=2] {'grid','col'}, dimensions={1} | all-to-all | bytes 7077888 | tf_op jit(solution)/shard_map/all_to_all | solution.py:86
  1171.8 8.3 all_to_all.32
  1180.1 10.9 convolution_multiply_fusion.1
  1190.9 0.0 reduce-scatter.2.cloned.1.call-update
  1191.0 637.2 %reduce-scatter.2.cloned.1.call-done = f32[8,256]{1,0:T(8,128)} async-done(((f32[1024,256]{1,0:T(8,128)}), f32[8,256]{1,0:T(8,128)}) %reduce-scatter.2.cloned.1.call-update) | async-done | bytes 8208 | tf_op jit(solution)/shard_map/reduce_scatter | solution.py:88
  (33 shorter events, 0.1 us)
Async XLA Ops:
  7.2 610.1 %copy-start = (bf16[1024,256]{1,0:T(8,128)(2,1)S(1)}, bf16[1024,256]{1,0:T(8,128)(2,1)}, u32[]{:S(2)}) copy-start(bf16[1024,256]{1,0:T(8,128)(2,1)} %param.7) | copy-start | bytes 1572868
  7.2 558.1 %all-reduce.3.cloned.1.call-start = ((), (), s32[]{:S(2)}) async-start(), calls=%async_computation.3 | async-start | bytes 2097152 | tf_op jit(solution)/shard_map/psum | solution.py:63
  638.1 94.2 %all-to-all-start = ((f32[128,2,6912]{2,1,0:T(2,128)}), f32[128,2,6912]{2,1,0:T(2,128)}, u32[]{:S(2)}, u32[]{:S(2)}) async-start(f32[128,2,6912]{2,1,0:T(2,128)} %all_to_all.26), calls=%async_computation | async-start | bytes 14155776 | tf_op jit(solution)/shard_map/all_to_all | solution.py:83
  647.7 1180.5 %reduce-scatter.2.cloned.1.call-start = ((), (), s32[]{:S(2)}) async-start(), calls=%async_computation.4 | async-start | bytes 1056768 | tf_op jit(solution)/shard_map/reduce_scatter | solution.py:88
  749.2 11.3 copy-start.6
  862.7 13.4 copy-start.5
  862.7 23.6 %slice-start = ((s8[4718592]{0:T(1024)(128)(4,1)}), s8[4194304]{0:T(1024)(128)(4,1)S(1)}, s32[]{:S(2)}) async-start(s8[4718592]{0:T(1024)(128)(4,1)} %bitcast.108), calls=%async_computation.5 | async-start | bytes 8388608
  876.1 10.2 slice-start.1
  897.6 25.7 %copy-start.2 = (f32[2,96,96,96]{1,3,2,0:T(8,128)}, f32[2,96,96,96]{1,3,2,0:T(8,128)S(1)}, u32[]{:S(2)}) copy-start(f32[2,96,96,96]{1,3,2,0:T(8,128)S(1)} %bitcast_multiply_fusion) | copy-start | bytes 21233668
  955.1 26.4 %copy-start.3 = (f32[2,96,96,96]{2,3,1,0:T(8,128)S(1)}, f32[2,96,96,96]{2,3,1,0:T(8,128)}, u32[]{:S(2)}) copy-start(f32[2,96,96,96]{2,3,1,0:T(8,128)} %copy.31) | copy-start | bytes 21233668
  955.1 50.1 %slice-start.2 = ((s8[9437184]{0:T(1024)(128)(4,1)}), s8[4194304]{0:T(1024)(128)(4,1)S(1)}, s32[]{:S(2)}) async-start(s8[9437184]{0:T(1024)(128)(4,1)} %bitcast.110), calls=%async_computation.7 | async-start | bytes 8388608
  955.2 50.1 %slice-start.3 = ((s8[9437184]{0:T(1024)(128)(4,1)}), s8[4194304]{0:T(1024)(128)(4,1)S(1)}, s32[]{:S(2)}) async-start(s8[9437184]{0:T(1024)(128)(4,1)} %bitcast.110), calls=%async_computation.8 | async-start | bytes 8388608
  955.2 50.1 %slice-start.5 = ((s8[9437184]{0:T(1024)(128)(4,1)}), s8[4194304]{0:T(1024)(128)(4,1)S(1)}, s32[]{:S(2)}) async-start(s8[9437184]{0:T(1024)(128)(4,1)} %bitcast.112), calls=%async_computation.10 | async-start | bytes 8388608
  955.2 50.1 %slice-start.6 = ((s8[9437184]{0:T(1024)(128)(4,1)}), s8[4194304]{0:T(1024)(128)(4,1)S(1)}, s32[]{:S(2)}) async-start(s8[9437184]{0:T(1024)(128)(4,1)} %bitcast.112), calls=%async_computation.11 | async-start | bytes 8388608
  981.6 23.7 %slice-start.4 = ((s8[9437184]{0:T(1024)(128)(4,1)}), s8[1048576]{0:T(1024)(128)(4,1)S(1)}, s32[]{:S(2)}) async-start(s8[9437184]{0:T(1024)(128)(4,1)} %bitcast.110), calls=%async_computation.9 | async-start | bytes 2097152
  981.6 23.7 %slice-start.7 = ((s8[9437184]{0:T(1024)(128)(4,1)}), s8[1048576]{0:T(1024)(128)(4,1)S(1)}, s32[]{:S(2)}) async-start(s8[9437184]{0:T(1024)(128)(4,1)} %bitcast.112), calls=%async_computation.12 | async-start | bytes 2097152
  1028.4 24.6 %copy-start.4 = (f32[2,96,96,96]{2,3,1,0:T(8,128)S(1)}, f32[2,96,96,96]{2,3,1,0:T(8,128)}, u32[]{:S(2)}) copy-start(f32[2,96,96,96]{2,3,1,0:T(8,128)} %copy.30) | copy-start | bytes 21233668
  1028.4 48.0 %slice-start.8 = ((s8[9437184]{0:T(1024)(128)(4,1)}), s8[4194304]{0:T(1024)(128)(4,1)S(1)}, s32[]{:S(2)}) async-start(s8[9437184]{0:T(1024)(128)(4,1)} %bitcast.114), calls=%async_computation.13 | async-start | bytes 8388608
  1028.4 48.0 %slice-start.9 = ((s8[9437184]{0:T(1024)(128)(4,1)}), s8[4194304]{0:T(1024)(128)(4,1)S(1)}, s32[]{:S(2)}) async-start(s8[9437184]{0:T(1024)(128)(4,1)} %bitcast.114), calls=%async_computation.14 | async-start | bytes 8388608
  1053.0 23.4 %slice-start.10 = ((s8[9437184]{0:T(1024)(128)(4,1)}), s8[1048576]{0:T(1024)(128)(4,1)S(1)}, s32[]{:S(2)}) async-start(s8[9437184]{0:T(1024)(128)(4,1)} %bitcast.114), calls=%async_computation.15 | async-start | bytes 2097152
  1171.8 656.4 %copy-start.1 = (bf16[1024,256]{1,0:T(8,128)(2,1)S(1)}, bf16[1024,256]{1,0:T(8,128)(2,1)}, u32[]{:S(2)}) copy-start(bf16[1024,256]{1,0:T(8,128)(2,1)} %param.7) | copy-start | bytes 1572868
Sparse Core Ops, SparseCore 0:
  16.1 549.1 all-reduce.2
  1191.1 637.0 reduce-scatter.1
